TPU v7x, 32 devices: a whole 2x2x4 slice. The times are simulated.
32 devices in a mesh: section: 4 (over x, core), doc: 2 (over y), mp: 4 (over z).
Axes of the slice: x: 2, y: 2, z: 4, core: 2. Of those that a mesh axis runs over, the one named last changes fastest.
Arguments:
- queries: bfloat16 [4, 512, 8, 4, 128], P('doc', None, 'section', 'mp'), may hold values from -420 to 420
- cotangent: bfloat16 [4, 512, 8, 4, 128], P('doc', None, 'section', 'mp'), may hold values from -180 to 180
- cache: bfloat16 [32, 128, 4, 2, 128], P('doc', 'section', 'mp'), may hold values from -7 to 7
- momentum: float32 [32, 128, 4, 2, 128], P('doc', 'section', 'mp'), may hold values from -3 to 3
- doc_lists: int32 [4, 8], P('doc'), may hold values from 0 to 31, as said below
- place: int32 [32], replicated, may hold values from 0 to 31, as said below
Outputs:
- attention: bfloat16 [4, 512, 8, 4, 128], P('doc', None, 'section', 'mp')
- new_cache: bfloat16 [32, 128, 4, 2, 128], P('doc', 'section', 'mp')
- new_momentum: float32 [32, 128, 4, 2, 128], P('doc', 'section', 'mp')
Inputs may be any that keep to these rules, and one draw needn't show every extreme that they name: `doc_lists`: the 2 rows of one index of doc (an aligned block of rows) name 16 different documents in all. Counting each document's owner as place[document] // 16, those documents lie on at most 8 per owner. `place`: each row of cache holds exactly one document.
All inputs are finite; a program needn't handle non-finite values.
Results may differ from a plain program's by a relative error of at most 0.017.
Values may be sent and summed in bfloat16 or wider, within the bound.
A program may use at most 64 MiB of HBM per device.

v0:
```python
import math

import jax
import jax.numpy as jnp
from jax import lax
from jax.sharding import PartitionSpec as P

momentum_decay = 0.9
step_rate = 0.3
clip_level = 0.5


def body(queries, cotangent, cache, momentum, doc_lists, place):
    rows_dev, seq_len, head_count, kv_count, head_size = queries.shape
    doc_dev, len_part = (cache.shape[0], cache.shape[1])
    doc_total = place.shape[0]
    owners = doc_total // doc_dev
    sections = lax.axis_size("section")
    list_len = doc_lists.shape[1]
    requests = rows_dev * list_len
    owner_used = min(owners, requests)
    capacity = (requests + owner_used - 1) // owner_used
    flat_width = kv_count * 2 * head_size
    score_scale = 1.0 / math.sqrt(head_size)
    everyone = lax.all_gather(doc_lists, "doc", axis=0, tiled=True).reshape(owners, requests)
    matches = (
        everyone[:, :, None] == jnp.arange(doc_total, dtype=jnp.int32)[None, None, :]
    ).astype(jnp.int32)
    positions = jnp.sum(matches * place[None, None, :], axis=-1)
    holder = positions // doc_dev
    local_slot = positions % doc_dev
    earlier = jnp.arange(requests)[:, None] > jnp.arange(requests)[None, :]
    same_owner = holder[:, :, None] == holder[:, None, :]
    slot_rank = jnp.sum((same_owner & earlier[None]).astype(jnp.int32), axis=-1)
    my_index = lax.axis_index("doc")
    my_holder = lax.dynamic_index_in_dim(holder, my_index, 0, keepdims=False)
    my_rank = lax.dynamic_index_in_dim(slot_rank, my_index, 0, keepdims=False)
    target = my_holder * capacity + my_rank
    claimed = (holder == my_index)[:, :, None] & (
        slot_rank[:, :, None] == jnp.arange(capacity)[None, None, :]
    )
    slot_table = jnp.sum(jnp.where(claimed, local_slot[:, :, None], 0), axis=1)
    filled = jnp.any(claimed, axis=1)
    stored = cache.reshape(doc_dev, len_part, flat_width)
    outgoing = jnp.where(filled[:, :, None, None], stored[slot_table], jnp.zeros((), jnp.bfloat16))
    fanned = jnp.broadcast_to(outgoing[None], (sections,) + outgoing.shape)
    fanned = fanned.reshape(sections * owners, capacity, len_part, flat_width)
    arrived = lax.all_to_all(fanned, ("section", "doc"), split_axis=0, concat_axis=0, tiled=True)
    arrived = arrived.reshape(sections, owners * capacity, len_part, flat_width)
    picked = arrived[:, target]
    fetched = jnp.moveaxis(picked, 0, 1).reshape(requests, sections * len_part, flat_width)
    length = fetched.shape[1]
    memory = fetched.reshape(rows_dev, list_len * length, kv_count, 2, head_size)

    def row_attention(operands):
        query_row, tangent_row, memory_row = operands
        query = query_row[:, :, 0, :].reshape(seq_len * head_count, head_size)
        tangent = tangent_row[:, :, 0, :].reshape(seq_len * head_count, head_size)
        key_rows = memory_row[:, 0, 0, :]
        value_rows = memory_row[:, 0, 1, :]
        scores = (
            jnp.einsum("qd,kd->qk", query, key_rows, preferred_element_type=jnp.float32)
            * score_scale
        )
        weights = jax.nn.softmax(scores, axis=-1)
        weight_bf = weights.astype(jnp.bfloat16)
        attended = jnp.dot(weight_bf, value_rows, preferred_element_type=jnp.float32).astype(
            jnp.bfloat16
        )
        row_delta = jnp.sum(
            attended.astype(jnp.float32) * tangent.astype(jnp.float32), axis=-1, keepdims=True
        )
        grad_weights = jnp.einsum(
            "qd,kd->qk", tangent, value_rows, preferred_element_type=jnp.float32
        )
        grad_scores = (weights * (grad_weights - row_delta) * score_scale).astype(jnp.bfloat16)
        grad_keys = jnp.einsum("qk,qd->kd", grad_scores, query, preferred_element_type=jnp.float32)
        grad_values = jnp.einsum(
            "qk,qd->kd", weight_bf, tangent, preferred_element_type=jnp.float32
        )
        grad_list = [jnp.stack([grad_keys, grad_values], axis=1).astype(jnp.bfloat16)]
        attended_list = [attended.reshape(seq_len, head_count, head_size)]
        return (jnp.stack(attended_list, axis=2), jnp.stack(grad_list, axis=1))

    attention, partial_value = lax.map(row_attention, (queries, cotangent, memory))
    partial_value = partial_value.reshape(requests, length, flat_width)
    pieces = partial_value.reshape(requests, sections, len_part, flat_width)
    parcel = (
        jnp.zeros((owners * capacity, sections, len_part, flat_width), jnp.bfloat16)
        .at[target]
        .set(pieces)
    )
    parcel = jnp.moveaxis(parcel, 1, 0).reshape(sections * owners, capacity, len_part, flat_width)
    returned = lax.all_to_all(parcel, ("section", "doc"), split_axis=0, concat_axis=0, tiled=True)
    returned = returned.reshape(sections, owners * capacity, len_part * flat_width).astype(
        jnp.float32
    )
    collected = jnp.sum(returned, axis=0)
    assign = (slot_table.reshape(-1)[None, :] == jnp.arange(doc_dev)[:, None]) & filled.reshape(-1)[
        None, :
    ]
    gradient = jnp.dot(
        assign.astype(jnp.float32),
        collected,
        precision=lax.Precision.HIGHEST,
        preferred_element_type=jnp.float32,
    )
    gradient = gradient.reshape(momentum.shape)
    norm_square = lax.psum(jnp.sum(gradient * gradient), ("section", "doc", "mp"))
    entry_count = doc_total * len_part * sections * kv_count * lax.axis_size("mp") * 2 * head_size
    clip_limit = clip_level * math.sqrt(entry_count)
    norm_value = jnp.sqrt(norm_square)
    factor = clip_limit / jnp.maximum(norm_value, clip_limit)
    new_momentum = momentum_decay * momentum + factor * gradient
    new_cache = (cache.astype(jnp.float32) - step_rate * new_momentum).astype(jnp.bfloat16)
    return (attention, new_cache, new_momentum)


def solution(mesh):
    in_specs = (
        P("doc", None, "section", "mp", None),
        P("doc", None, "section", "mp", None),
        P("doc", "section", "mp", None, None),
        P("doc", "section", "mp", None, None),
        P("doc", None),
        P(),
    )
    out_specs = (
        P("doc", None, "section", "mp", None),
        P("doc", "section", "mp", None, None),
        P("doc", "section", "mp", None, None),
    )
    return jax.shard_map(body, mesh=mesh, in_specs=in_specs, out_specs=out_specs, check_vma=False)
```

profile of v0, /device:TPU:0, one launch (start us, length us, event | category | flops | bytes accessed | tf_op | source)
XLA Modules:
  0.0 125.7 jit_solution(9114771559065635696)
XLA Ops:
  0.7 5.4 %all-gather = s32[2,2,8]{2,1,0:T(2,128)S(1)} all-gather(s32[1,2,8]{2,1,0:T(2,128)} %bitcast.90), channel_id=1, replica_groups=mesh['section'=4,'doc'=2,'mp'=4] {'doc'}, dimensions={0}, use_global_device_ids=true | all-gather | bytes 192 | tf_op jit(solution)/shard_map/all_gather | solution.py:25
  6.2 0.8 select_reduce_fusion
  7.0 0.2 convert_reduce_fusion
  7.2 0.2 fusion.14
  7.4 0.2 select_reduce_fusion.1
  7.6 1.1 reshape.196
  8.8 0.6 gather_fusion
  9.3 0.1 broadcast_select_fusion
  9.4 1.1 broadcast_in_dim.47
  10.6 4.2 %all-to-all-start = ((bf16[8,8,32,256]{3,2,1,0:T(8,128)(2,1)}), bf16[8,8,32,256]{3,2,1,0:T(8,128)(2,1)S(1)}, u32[]{:S(2)}, u32[]{:S(2)}) async-start(bf16[8,8,32,256]{3,2,1,0:T(8,128)(2,1)} %bitcast.11), calls=%async_computation | async-start | bytes 2097152 | tf_op jit(solution)/shard_map/all_to_all | solution.py:48
  14.8 14.5 %all-to-all-done = bf16[8,8,32,256]{3,2,1,0:T(8,128)(2,1)S(1)} async-done(((bf16[8,8,32,256]{3,2,1,0:T(8,128)(2,1)}), bf16[8,8,32,256]{3,2,1,0:T(8,128)(2,1)S(1)}, u32[]{:S(2)}, u32[]{:S(2)}) %all-to-all-start) | async-done | bytes 1048608 | tf_op jit(solution)/shard_map/all_to_all | solution.py:48
  29.3 0.6 gather_fusion.1
  29.9 0.3 reshape_reshape.6
  30.2 28.1 %while.12 = (s32[]{:T(128)}, bf16[2,512,2,1,128]{4,2,1,3,0:T(2,128)(2,1)}, bf16[2,1024,1,2,128]{4,3,1,0,2:T(2,128)(2,1)}, bf16[2,512,2,1,128]{4,2,3,1,0:T(2,128)...) while((s32[]{:T(128)}, ...), condition=%wide.region_8.9_spmd, body=%wide.region_4.8_spmd.sunk | while | flops 1364325376 | bytes 54833840 | solution.py:85
  30.2 0.4 constant_dynamic-slice_fusion.7
  30.7 0.2 constant_dynamic-slice_fusion.8
  30.9 0.7 multiply_reduce_fusion.5
  31.6 0.7 fusion.39
  32.4 1.3 %constant_dynamic-slice_fusion.6 = bf16[1,512,2,1,128]{4,2,1,3,0:T(2,128)(2,1)S(1)} fusion(bf16[2,512,2,1,128]{4,2,1,3,0:T(2,128)(2,1)} %get-tuple-element.169, s32[]{:T(128)} %get-tuple-element.157), kind=kLoop, calls=%fused_computation.23.clone.1 | loop fusion | bytes 524292 | tf_op jit(solution)/shard_map/while/body/jit(dynamic_index_in_dim)/dynamic_slice | solution.py:85
  33.7 1.3 multiply_reduce_fusion.6
  35.0 3.6 %fusion.41 = bf16[1,1024,1,1,128]{4,1,3,2,0:T(8,128)(2,1)S(1)} fusion(bf16[1024,128]{1,0:T(8,128)(2,1)S(1)} %bitcast.82, bf16[1024,128]{1,0:T(8,128)(2,1)S(1)} %bitcast.86, f32[1024]{0:T(1024)S(1)} %get-tuple-element.149, bf16[1024,1,2,128]{3,0,2,1:T(8,128)(2,1)S(1)} %bitcast.80, f32[1024,1024]{0,1:T(8,128)} %copy-done, f32[1024]{0:T(1024)S(1)} %fusion.39, ...), kind=kOutput, calls=%fused_computation.12.clone.1 | convolution fusion | flops 544342016 | bytes 5255168 | tf_op jit(solution)/shard_map/while/body/eval_jaxpr/qk,qd->kd/dot_general | solution.py:77
  38.6 3.2 %fusion.40 = bf16[1,1024,1,1,128]{4,1,3,2,0:T(8,128)(2,1)S(1)} fusion(bf16[1024,128]{1,0:T(8,128)(2,1)S(1)} %bitcast.87, f32[1024,1024]{0,1:T(8,128)} %copy-done, f32[1024]{0:T(1024)S(1)} %fusion.39, f32[1024]{0:T(1024)S(1)} %get-tuple-element.147), kind=kOutput, calls=%fused_computation.13.clone.1 | convolution fusion | flops 272760832 | bytes 4726784 | tf_op jit(solution)/shard_map/while/body/eval_jaxpr/qk,qd->kd/dot_general | solution.py:78
  41.8 0.6 copy_dynamic-update-slice_fusion.2
  42.4 1.0 copy-done.3
  43.4 0.9 constant_dynamic-update-slice_fusion.2
  44.3 0.4 constant_dynamic-slice_fusion.7
  44.7 0.2 constant_dynamic-slice_fusion.8
  44.9 0.7 multiply_reduce_fusion.5
  45.7 0.7 fusion.39
  46.4 1.3 %constant_dynamic-slice_fusion.6 = bf16[1,512,2,1,128]{4,2,1,3,0:T(2,128)(2,1)S(1)} fusion(bf16[2,512,2,1,128]{4,2,1,3,0:T(2,128)(2,1)} %get-tuple-element.169, s32[]{:T(128)} %get-tuple-element.157), kind=kLoop, calls=%fused_computation.23.clone.1 | loop fusion | bytes 524292 | tf_op jit(solution)/shard_map/while/body/jit(dynamic_index_in_dim)/dynamic_slice | solution.py:85
  47.7 1.3 %multiply_reduce_fusion.6 = (f32[1024]{0:T(1024)S(1)}, bf16[1024,128]{1,0:T(8,128)(2,1)S(1)}) fusion(bf16[1024,128]{1,0:T(8,128)(2,1)S(1)} %bitcast.85, bf16[1024,1,2,128]{3,0,2,1:T(8,128)(2,1)S(1)} %bitcast.79, f32[1024]{0:T(1024)S(1)} %fusion.39, f32[1024]{0:T(1024)S(1)} %get-tuple-element.147, f32[1024,1024]{0,1:T(8,128)S(1)} %get-tuple-element.146), kind=kOutput, calls=%fused_computation.19.clone.1 | convolution fusion | flops 273284096 | bytes 4993024 | tf_op jit(solution)/shard_map/while/body/eval_jaxpr/dot_general | solution.py:67
  49.0 3.6 %fusion.41 = bf16[1,1024,1,1,128]{4,1,3,2,0:T(8,128)(2,1)S(1)} fusion(bf16[1024,128]{1,0:T(8,128)(2,1)S(1)} %bitcast.82, bf16[1024,128]{1,0:T(8,128)(2,1)S(1)} %bitcast.86, f32[1024]{0:T(1024)S(1)} %get-tuple-element.149, bf16[1024,1,2,128]{3,0,2,1:T(8,128)(2,1)S(1)} %bitcast.80, f32[1024,1024]{0,1:T(8,128)} %copy-done, f32[1024]{0:T(1024)S(1)} %fusion.39, ...), kind=kOutput, calls=%fused_computation.12.clone.1 | convolution fusion | flops 544342016 | bytes 5255168 | tf_op jit(solution)/shard_map/while/body/eval_jaxpr/qk,qd->kd/dot_general | solution.py:77
  52.6 3.2 %fusion.40 = bf16[1,1024,1,1,128]{4,1,3,2,0:T(8,128)(2,1)S(1)} fusion(bf16[1024,128]{1,0:T(8,128)(2,1)S(1)} %bitcast.87, f32[1024,1024]{0,1:T(8,128)} %copy-done, f32[1024]{0:T(1024)S(1)} %fusion.39, f32[1024]{0:T(1024)S(1)} %get-tuple-element.147), kind=kOutput, calls=%fused_computation.13.clone.1 | convolution fusion | flops 272760832 | bytes 4726784 | tf_op jit(solution)/shard_map/while/body/eval_jaxpr/qk,qd->kd/dot_general | solution.py:78
  55.9 0.6 copy_dynamic-update-slice_fusion.2
  56.5 1.0 copy-done.3
  57.5 0.9 constant_dynamic-update-slice_fusion.2
  58.3 1.7 %reshape.221 = bf16[16,4,32,256]{3,2,1,0:T(8,128)(2,1)S(1)} reshape(bf16[2,1024,1,2,128]{4,3,1,0,2:T(2,128)(2,1)} %get-tuple-element.37) | data formatting | bytes 2097152 | tf_op jit(solution)/shard_map/reshape;reshape | solution.py:87
  60.1 0.1 broadcast_in_dim.48
  60.2 1.1 scatter_fusion
  61.3 1.1 copy.34
  62.4 3.6 %all-to-all-start.1 = ((bf16[8,8,32,256]{3,2,1,0:T(8,128)(2,1)}), bf16[8,8,32,256]{3,2,1,0:T(8,128)(2,1)S(1)}, u32[]{:S(2)}, u32[]{:S(2)}) async-start(bf16[8,8,32,256]{3,2,1,0:T(8,128)(2,1)} %bitcast.18), calls=%async_computation.1 | async-start | bytes 2097152 | tf_op jit(solution)/shard_map/all_to_all | solution.py:94
  66.2 14.3 %all-to-all-done.1 = bf16[8,8,32,256]{3,2,1,0:T(8,128)(2,1)S(1)} async-done(((bf16[8,8,32,256]{3,2,1,0:T(8,128)(2,1)}), bf16[8,8,32,256]{3,2,1,0:T(8,128)(2,1)S(1)}, u32[]{:S(2)}, u32[]{:S(2)}) %all-to-all-start.1) | async-done | bytes 1048608 | tf_op jit(solution)/shard_map/all_to_all | solution.py:94
  80.5 0.4 reshape.200
  80.9 0.1 reduce_sum.69
  81.1 1.0 multiply_reduce_fusion.2
  82.1 39.8 %psum.7 = f32[]{:T(128)} all-reduce(f32[]{:T(128)} %get-tuple-element.103), channel_id=1, replica_groups=mesh['section'=4,'doc'=2,'mp'=4] {'section','doc','mp'}, use_global_device_ids=true, to_apply=%region_12.13 | all-reduce | flops 1 | bytes 8 | tf_op jit(solution)/shard_map/psum | solution.py:109
  122.6 0.4 mul.74
  123.1 2.6 %subtract_convert_fusion = (bf16[16,32,1,2,128]{4,3,2,1,0:T(2,128)(2,1)}, f32[16,32,1,2,128]{4,3,2,1,0:T(2,128)}) fusion(bf16[16,32,1,2,128]{4,3,2,1,0:T(2,128)(2,1)S(1)} %copy-done.4, f32[16,32,1,2,128]{4,3,1,0,2:T(2,128)S(1)} %mul.74, f32[16,32,1,2,128]{4,3,2,1,0:T(2,128)} %param.11), kind=kLoop, calls=%fused_computation.29 | loop fusion | flops 786432 | bytes 2097152 | tf_op jit(solution)/shard_map/convert_element_type | solution.py:115
  (32 shorter events, 0.7 us)
Async XLA Ops:
  9.3 20.9 %copy-start.1 = (bf16[2,512,2,1,128]{4,2,3,1,0:T(2,128)(2,1)S(1)}, bf16[2,512,2,1,128]{4,2,3,1,0:T(2,128)(2,1)}, u32[]{:S(2)}) copy-start(bf16[2,512,2,1,128]{4,2,3,1,0:T(2,128)(2,1)} %param.8) | copy-start | bytes 1572868
  10.6 18.7 %all-to-all-start = ((bf16[8,8,32,256]{3,2,1,0:T(8,128)(2,1)}), bf16[8,8,32,256]{3,2,1,0:T(8,128)(2,1)S(1)}, u32[]{:S(2)}, u32[]{:S(2)}) async-start(bf16[8,8,32,256]{3,2,1,0:T(8,128)(2,1)} %bitcast.11), calls=%async_computation | async-start | bytes 2097152 | tf_op jit(solution)/shard_map/all_to_all | solution.py:48
  31.6 3.3 %copy-start = (f32[1024,1024]{0,1:T(8,128)}, f32[1024,1024]{0,1:T(8,128)S(1)}, u32[]{:S(2)}) copy-start(f32[1024,1024]{0,1:T(8,128)S(1)} %get-tuple-element.146) | copy-start | bytes 12582916 | tf_op jit(solution)/shard_map/while
  38.6 3.3 %copy-start.2 = (bf16[2,1024,1,2,128]{4,3,1,0,2:T(2,128)(2,1)S(1)}, bf16[2,1024,1,2,128]{4,3,1,0,2:T(2,128)(2,1)}, u32[]{:S(2)}) copy-start(bf16[2,1024,1,2,128]{4,3,1,0,2:T(2,128)(2,1)} %get-tuple-element.159) | copy-start | bytes 3145732 | tf_op jit(solution)/shard_map/while
  42.4 1.0 copy-start.3
  45.6 3.3 %copy-start = (f32[1024,1024]{0,1:T(8,128)}, f32[1024,1024]{0,1:T(8,128)S(1)}, u32[]{:S(2)}) copy-start(f32[1024,1024]{0,1:T(8,128)S(1)} %get-tuple-element.146) | copy-start | bytes 12582916 | tf_op jit(solution)/shard_map/while
  52.6 3.3 %copy-start.2 = (bf16[2,1024,1,2,128]{4,3,1,0,2:T(2,128)(2,1)S(1)}, bf16[2,1024,1,2,128]{4,3,1,0,2:T(2,128)(2,1)}, u32[]{:S(2)}) copy-start(bf16[2,1024,1,2,128]{4,3,1,0,2:T(2,128)(2,1)} %get-tuple-element.159) | copy-start | bytes 3145732 | tf_op jit(solution)/shard_map/while
  56.5 1.0 copy-start.3
  62.4 18.0 %all-to-all-start.1 = ((bf16[8,8,32,256]{3,2,1,0:T(8,128)(2,1)}), bf16[8,8,32,256]{3,2,1,0:T(8,128)(2,1)S(1)}, u32[]{:S(2)}, u32[]{:S(2)}) async-start(bf16[8,8,32,256]{3,2,1,0:T(8,128)(2,1)} %bitcast.18), calls=%async_computation.1 | async-start | bytes 2097152 | tf_op jit(solution)/shard_map/all_to_all | solution.py:94
  66.2 56.9 %copy-start.4 = (bf16[16,32,1,2,128]{4,3,2,1,0:T(2,128)(2,1)S(1)}, bf16[16,32,1,2,128]{4,3,2,1,0:T(2,128)(2,1)}, u32[]{:S(2)}) copy-start(bf16[16,32,1,2,128]{4,3,2,1,0:T(2,128)(2,1)} %param.10) | copy-start | bytes 786436
where the time goes:
time: 126 us
  blocking collectives  45.2 us (36%)
  waiting for transfers between devices  28.8 us (23%)
  matrix products  18.6 us (15%)
  local copies, waits for them, and re-layouts  17.8 us (14%)
  starting transfers between devices  7.74 us (6%)
  other arithmetic  5.8 us (5%)
  between operations  1.54 us (1%)
    psum x1, blocking collectives, body(): lax.psum(jnp.sum(gradient * gradient), ('section', 'doc', 'mp'))  39.8 us
    all_to_all x1, waiting for transfers between devices, body(): lax.all_to_all(fanned, ('section', 'doc'), split_axis=0, concat_axis=0, t...  14.5 us
    all_to_all x1, waiting for transfers between devices, body(): lax.all_to_all(parcel, ('section', 'doc'), split_axis=0, concat_axis=0, t...  14.3 us
    dot_general x2, matrix products, row_attention(): jnp.einsum('qk,qd->kd', grad_scores, query, preferred_element_type=jnp.fl...  7.19 us
    dot_general x2, matrix products, row_attention(): jnp.einsum('qk,qd->kd', weight_bf, tangent, preferred_element_type=jnp.fl...  6.4 us
    all_gather x1, blocking collectives, body(): lax.all_gather(doc_lists, 'doc', axis=0, tiled=True)  5.44 us
    all_to_all x1, starting transfers between devices, body(): lax.all_to_all(fanned, ('section', 'doc'), split_axis=0, concat_axis=0, t...  4.18 us
    dynamic_slice x8, local copies, waits for them, and re-layouts, body(): lax.map(row_attention, (queries, cotangent, memory))  3.91 us
  transfers between devices with their start and end apart: 2, of which 2 were waited for; matrix products, arithmetic and copies ran while one was open for 0% of the time, Pallas kernels for 0%

commit v1 on v0

v1 whole, which is shorter than its diff:
```python
import functools
import math

import jax
import jax.numpy as jnp
from jax import lax
from jax.experimental import pallas as pl
from jax.experimental.pallas import tpu as pltpu
from jax.sharding import PartitionSpec as P

momentum_decay = 0.9
step_rate = 0.3
clip_level = 0.5
MESH = pl.DeviceIdType.MESH


def nt(a, b):
    return lax.dot_general(a, b, (((1,), (1,)), ((), ())), preferred_element_type=jnp.float32)


def mm(a, b):
    return jnp.dot(a, b, preferred_element_type=jnp.float32)


def kernel(
    cfg,
    lists_ref, place_ref, q_ref, t_ref, cache_ref, mom_ref,
    att_ref, newc_ref, newm_ref,
    mypos, allpos, tab, target, inverse,
    posvm, wide, kvc, arr, outbuf, keys, vals, valt, dk, dv,
    keep, snd, rcv, parcel, ret, part1, part2,
    pos_send, pos_recv, loc_sem, dir_send, arr_recv, fwd_send,
    sib_send, sib_recv, ret_send, ret_recv, n1_send, n1_recv, n2_send, n2_recv,
):
    sections, owners, mps, cap, doc_dev, len_part, rows, list_len, clip_limit, score_scale = cfg
    low = 2 if sections % 2 == 0 else 1
    high = sections // low
    requests = rows * list_len
    head = q_ref.shape[-1]
    sec = lax.axis_index("section")
    doc = lax.axis_index("doc")
    mp = lax.axis_index("mp")
    hi = sec // low
    lo = sec % low

    def rot(base, step, size):
        return lax.rem(base + step, size)

    group = [(a, b) for a in range(sections) for b in range(owners) if (a, b) != (0, 0)]
    peers = [(a, b) for a in range(high) for b in range(owners) if (a, b) != (0, 0)]
    barrier = pltpu.get_barrier_semaphore()
    for a, b in group:
        pl.semaphore_signal(
            barrier, inc=1,
            device_id={"section": rot(sec, a, sections), "doc": rot(doc, b, owners), "mp": mp},
            device_id_type=MESH,
        )
    for c in range(1, mps):
        pl.semaphore_signal(
            barrier, inc=1, device_id={"section": sec, "doc": doc, "mp": rot(mp, c, mps)},
            device_id_type=MESH,
        )

    def to(s, d):
        return {"section": s, "doc": d, "mp": mp}

    def remote(src, dst, ssem, rsem, dev):
        return pltpu.make_async_remote_copy(
            src_ref=src, dst_ref=dst, send_sem=ssem, recv_sem=rsem, device_id=dev,
            device_id_type=MESH,
        )

    count = doc_dev * len_part
    wide[0 : 2 * count, :] = cache_ref[...].astype(jnp.float32)
    kvc[:, 0] = wide[pl.ds(0, count, stride=2), :].astype(jnp.bfloat16).reshape(doc_dev, len_part, head)
    kvc[:, 1] = wide[pl.ds(1, count, stride=2), :].astype(jnp.bfloat16).reshape(doc_dev, len_part, head)

    lane = lax.broadcasted_iota(jnp.int32, (8, 128), 1)
    vec = jnp.zeros((8, 128), jnp.int32)
    places = []
    for r in range(requests):
        where = place_ref[lists_ref[r // list_len, r % list_len]]
        places.append(where)
        vec = jnp.where(lane == r, where, vec)
    posvm[doc] = vec

    def slots(get, d):
        found = [jnp.int32(-1)] * cap
        seen = jnp.int32(0)
        for r in range(requests):
            where = get(r)
            mine = (where // doc_dev) == doc
            local = where % doc_dev
            for c in range(min(cap, r + 1)):
                found[c] = jnp.where(mine & (seen == c), local, found[c])
            seen = seen + mine.astype(jnp.int32)
        for c in range(cap):
            tab[d * cap + c] = found[c]
        return found

    pl.semaphore_wait(barrier, len(group) + mps - 1)

    pos_copies = []
    for b in range(1, owners):
        cp = remote(posvm.at[doc], posvm.at[doc], pos_send.at[b], pos_recv.at[doc], to(sec, rot(doc, b, owners)))
        cp.start()
        pos_copies.append(cp)

    sends = []
    sib = hi * low + rot(lo, 1, low)

    def block(s, d):
        return arr.at[s, pl.ds(d * cap, cap)]

    def forward(h, d):
        if low == 1:
            return
        s = h * low + lo
        cp = remote(block(s, d), block(s, d), fwd_send.at[h, d], arr_recv.at[s, d], to(sib, doc))
        cp.start()
        sends.append(cp)

    found = slots(lambda r: places[r], doc)
    for c in range(cap):
        arr[sec, doc * cap + c] = kvc[jnp.maximum(found[c], 0)]
    for a in range(1, high):
        h = rot(hi, a, high)
        cp = remote(block(sec, doc), block(sec, doc), dir_send.at[a, 0], arr_recv.at[sec, doc], to(h * low + lo, doc))
        cp.start()
        sends.append(cp)
    forward(hi, doc)

    for b in range(1, owners):
        d = rot(doc, b, owners)
        remote(posvm.at[d], posvm.at[d], pos_send.at[b], pos_recv.at[d], to(sec, d)).wait_recv()
        local = pltpu.make_async_copy(posvm.at[d], allpos.at[d], loc_sem)
        local.start()
        local.wait()
        found = slots(lambda r: allpos[d, 0, r], d)
        for c in range(cap):
            outbuf[b, c] = kvc[jnp.maximum(found[c], 0)]
        for a in range(high):
            h = rot(hi, a, high)
            cp = remote(outbuf.at[b], block(sec, doc), dir_send.at[a, b], arr_recv.at[sec, doc], to(h * low + lo, d))
            cp.start()
            sends.append(cp)

    targets = []
    for r in range(requests):
        rank = jnp.int32(0)
        for e in range(r):
            rank = rank + ((places[e] // doc_dev) == (places[r] // doc_dev)).astype(jnp.int32)
        targets.append((places[r] // doc_dev) * cap + rank)
        target[r] = targets[r]
    for i in range(owners * cap):
        who = jnp.int32(0)
        for r in range(requests):
            who = jnp.where(targets[r] == i, r, who)
        inverse[i] = who

    for a, b in peers:
        h, d = rot(hi, a, high), rot(doc, b, owners)
        s = h * low + lo
        remote(block(s, d), block(s, d), dir_send.at[a, b], arr_recv.at[s, d], to(s, d)).wait_recv()
        forward(h, d)
    if low > 1:
        for a in range(high):
            for b in range(owners):
                h, d = rot(hi, a, high), rot(doc, b, owners)
                s = h * low + rot(lo, 1, low)
                remote(block(s, d), block(s, d), fwd_send.at[h, d], arr_recv.at[s, d], to(s, d)).wait_recv()

    seq = q_ref.shape[1]
    tile = 256 if seq % 256 == 0 else seq
    exp_scale = score_scale * math.log2(math.e)
    shape5 = (list_len, high, low, len_part, head)
    key_count = list_len * sections * len_part
    for row in range(rows):
        for i in range(list_len):
            slot = target[row * list_len + i]
            for s in range(sections):
                at = (i * sections + s) * len_part
                piece = arr[s, slot]
                keys[at : at + len_part, :] = piece[0]
                vals[at : at + len_part, :] = piece[1]
        valt[...] = vals[...].T
        dk[...] = jnp.zeros_like(dk)
        dv[...] = jnp.zeros_like(dv)

        def step(j, carry):
            at = pl.ds(pl.multiple_of(j * tile, tile), tile)
            q = q_ref[row, at, :]
            t = t_ref[row, at, :]
            scores = nt(keys[...], q)
            top = jnp.max(scores, axis=0, keepdims=True)
            power = jnp.exp2((scores - top) * exp_scale)
            weights = power * (1.0 / jnp.sum(power, axis=0, keepdims=True))
            weight_bf = weights.astype(jnp.bfloat16)
            attended = mm(valt[...], weight_bf).astype(jnp.bfloat16).astype(jnp.float32)
            att_ref[row, at, :] = attended.T.astype(jnp.bfloat16)
            delta = jnp.sum(attended * t.astype(jnp.float32).T, axis=0, keepdims=True)
            grad = (weights * (nt(vals[...], t) - delta)).astype(jnp.bfloat16)
            dk[...] += mm(grad, q).reshape(shape5)
            dv[...] += mm(weight_bf, t).reshape(shape5)
            return carry

        lax.fori_loop(0, seq // tile, step, 0)
        span = pl.ds(row * list_len, list_len)
        for h in range(high):
            keep[span, h, 0] = dk[:, h, lo] * score_scale
            keep[span, h, 1] = dv[:, h, lo]
            if low > 1:
                snd[span, h, 0] = (dk[:, h, rot(lo, 1, low)] * score_scale).astype(jnp.bfloat16)
                snd[span, h, 1] = dv[:, h, rot(lo, 1, low)].astype(jnp.bfloat16)
        if low > 1:
            cp = remote(snd.at[span], rcv.at[span], sib_send.at[row], sib_recv.at[row], to(sib, doc))
            cp.start()
            sends.append(cp)

    if low > 1:
        for row in range(rows):
            span = pl.ds(row * list_len, list_len)
            remote(snd.at[span], rcv.at[span], sib_send.at[row], sib_recv.at[row], to(sib, doc)).wait_recv()

    def total(request, h):
        value = keep[request, h]
        if low > 1:
            value = value + rcv[request, h].astype(jnp.float32)
        return value.astype(jnp.bfloat16)

    def slot_block(h, d):
        return ret.at[h, pl.ds(d * cap, cap)]

    for a, b in peers[::-1]:
        h, d = rot(hi, a, high), rot(doc, b, owners)
        for c in range(cap):
            parcel[a, b, c] = total(inverse[d * cap + c], h)
        cp = remote(parcel.at[a, b], slot_block(hi, doc), ret_send.at[a, b], ret_recv.at[hi, doc], to(h * low + lo, d))
        cp.start()
        sends.append(cp)
    for c in range(cap):
        ret[hi, doc * cap + c] = total(inverse[doc * cap + c], hi)
    for a, b in peers:
        h, d = rot(hi, a, high), rot(doc, b, owners)
        remote(parcel.at[a, b], slot_block(h, d), ret_send.at[a, b], ret_recv.at[h, d], to(h * low + lo, d)).wait_recv()

    def gather(p, square):
        value = jnp.zeros((2, len_part, head), jnp.float32)
        for d in range(owners):
            pick = jnp.int32(0)
            named = jnp.float32(0.0)
            for c in range(cap):
                same = tab[d * cap + c] == p
                pick = jnp.where(same, c, pick)
                named = jnp.where(same, jnp.float32(1.0), named)
            both = ret[0, d * cap + pick].astype(jnp.float32)
            for h in range(1, high):
                both = both + ret[h, d * cap + pick].astype(jnp.float32)
            value = value + jnp.where(named > 0.5, both, 0.0)
        base = p * 2 * len_part
        wide[pl.ds(base, len_part, stride=2), :] = value[0]
        wide[pl.ds(base + 1, len_part, stride=2), :] = value[1]
        return square + jnp.sum((value * value).reshape(-1, 8, head), axis=0)

    square = lax.fori_loop(0, doc_dev, gather, jnp.zeros((8, head), jnp.float32))

    part1[sec * owners + doc] = square
    for n, (a, b) in enumerate(group):
        s, d = rot(sec, a, sections), rot(doc, b, owners)
        mine = part1.at[sec * owners + doc]
        cp = remote(mine, mine, n1_send.at[n], n1_recv.at[sec * owners + doc], to(s, d))
        cp.start()
        sends.append(cp)
    for n, (a, b) in enumerate(group):
        s, d = rot(sec, a, sections), rot(doc, b, owners)
        other = part1.at[s * owners + d]
        remote(other, other, n1_send.at[n], n1_recv.at[s * owners + d], to(s, d)).wait_recv()
    part2[mp] = jnp.sum(part1[...], axis=0)
    for c in range(1, mps):
        cp = remote(part2.at[mp], part2.at[mp], n2_send.at[c], n2_recv.at[mp], {"section": sec, "doc": doc, "mp": rot(mp, c, mps)})
        cp.start()
        sends.append(cp)
    for c in range(1, mps):
        m = rot(mp, c, mps)
        remote(part2.at[m], part2.at[m], n2_send.at[c], n2_recv.at[m], {"section": sec, "doc": doc, "mp": m}).wait_recv()
    whole = jnp.sum(part2[...], axis=0)
    whole = jnp.sum(jnp.sum(whole, axis=0, keepdims=True), axis=1, keepdims=True)
    factor = clip_limit / jnp.maximum(jnp.sqrt(whole), clip_limit)
    fresh = momentum_decay * mom_ref[...] + factor * wide[0 : 2 * count, :]
    newm_ref[...] = fresh
    newc_ref[...] = (cache_ref[...].astype(jnp.float32) - step_rate * fresh).astype(jnp.bfloat16)
    for cp in pos_copies + sends:
        cp.wait_send()


def body(queries, cotangent, cache, momentum, doc_lists, place):
    rows, seq_len, heads, kv_count, head = queries.shape
    doc_dev, len_part = cache.shape[:2]
    doc_total = place.shape[0]
    owners = doc_total // doc_dev
    sections = lax.axis_size("section")
    mps = lax.axis_size("mp")
    list_len = doc_lists.shape[1]
    requests = rows * list_len
    used = min(owners, requests)
    cap = (requests + used - 1) // used
    low = 2 if sections % 2 == 0 else 1
    high = sections // low
    entry_count = doc_total * len_part * sections * kv_count * mps * 2 * head
    clip_limit = clip_level * math.sqrt(entry_count)
    cfg = (sections, owners, mps, cap, doc_dev, len_part, rows, list_len, clip_limit, 1.0 / math.sqrt(head))
    f32, bf16, i32 = jnp.float32, jnp.bfloat16, jnp.int32
    key_count = list_len * sections * len_part
    flat = 2 * doc_dev * len_part
    vm, dma = pltpu.VMEM, pltpu.SemaphoreType.DMA
    shape5 = (list_len, high, low, len_part, head)
    piece = (2, len_part, head)
    vmem = pl.BlockSpec(memory_space=pltpu.VMEM)
    smem = pl.BlockSpec(memory_space=pltpu.SMEM)
    queries_flat = queries.reshape(rows, seq_len * heads, head)
    att, newc, newm = pl.pallas_call(
        functools.partial(kernel, cfg),
        out_shape=(
            jax.ShapeDtypeStruct(queries_flat.shape, bf16),
            jax.ShapeDtypeStruct((flat, head), bf16),
            jax.ShapeDtypeStruct((flat, head), f32),
        ),
        in_specs=[smem, smem, vmem, vmem, vmem, vmem],
        out_specs=(vmem, vmem, vmem),
        scratch_shapes=[
            pltpu.SMEM((requests,), i32),
            pltpu.SMEM((owners, 8, 128), i32),
            pltpu.SMEM((owners * cap,), i32),
            pltpu.SMEM((requests,), i32),
            pltpu.SMEM((owners * cap,), i32),
            vm((owners, 8, 128), i32),
            vm((flat + 8, head), f32),
            vm((doc_dev,) + piece, bf16),
            vm((sections, owners * cap) + piece, bf16),
            vm((owners, cap) + piece, bf16),
            vm((key_count, head), bf16),
            vm((key_count, head), bf16),
            vm((head, key_count), bf16),
            vm(shape5, f32),
            vm(shape5, f32),
            vm((requests, high) + piece, f32),
            vm((requests, high) + piece, bf16),
            vm((requests, high) + piece, bf16),
            vm((high, owners, cap) + piece, bf16),
            vm((high, owners * cap) + piece, bf16),
            vm((sections * owners, 8, head), f32),
            vm((mps, 8, head), f32),
            dma((owners,)),
            dma((owners,)),
            dma,
            dma((high, owners)),
            dma((sections, owners)),
            dma((high, owners)),
            dma((rows,)),
            dma((rows,)),
            dma((high, owners)),
            dma((high, owners)),
            dma((sections * owners,)),
            dma((sections * owners,)),
            dma((mps,)),
            dma((mps,)),
        ],
        compiler_params=pltpu.CompilerParams(
            collective_id=0, has_side_effects=True, vmem_limit_bytes=48 * 1024 * 1024
        ),
        cost_estimate=pl.CostEstimate(
            flops=10 * rows * seq_len * heads * key_count * head,
            bytes_accessed=4 * 1024 * 1024,
            transcendentals=rows * seq_len * heads * key_count,
        ),
    )(
        doc_lists,
        place,
        queries_flat,
        cotangent.reshape(queries_flat.shape),
        cache.reshape(flat, head),
        momentum.reshape(flat, head),
    )
    return att.reshape(queries.shape), newc.reshape(cache.shape), newm.reshape(momentum.shape)


def solution(mesh):
    in_specs = (
        P("doc", None, "section", "mp", None),
        P("doc", None, "section", "mp", None),
        P("doc", "section", "mp", None, None),
        P("doc", "section", "mp", None, None),
        P("doc", None),
        P(),
    )
    out_specs = (
        P("doc", None, "section", "mp", None),
        P("doc", "section", "mp", None, None),
        P("doc", "section", "mp", None, None),
    )
    return jax.shard_map(body, mesh=mesh, in_specs=in_specs, out_specs=out_specs, check_vma=False)
```

time: 126 us -> 54.3 us (0.43)
  Pallas kernels: 0 us -> 46.3 us
  blocking collectives: 45.2 us -> 0 us
  waiting for transfers between devices: 28.8 us -> 0 us
  matrix products: 18.6 us -> 0 us
  local copies, waits for them, and re-layouts: 17.8 us -> 7.03 us
  starting transfers between devices: 7.74 us -> 0 us
  other arithmetic: 5.8 us -> 0 us
    pallas_call x0 -> x1, Pallas kernels: none -> 46.3 us  [body(): pl.pallas_call(functools.partial(kernel, cfg), out_shape=(jax.ShapeDtypeS...]
    psum x1 -> x0, blocking collectives: 39.8 us -> none  [body(): lax.psum(jnp.sum(gradient * gradient), ('section', 'doc', 'mp'))]
    all_to_all x2 -> x0, waiting for transfers between devices: 28.8 us -> none  [the longest x1 14.5 us: body(): lax.all_to_all(fanned, ('section', 'doc'), split_axis=0, concat_axis=0, t...]
    dot_general x9 -> x0, matrix products: 18.6 us -> none  [the longest x2 7.19 us: row_attention(): jnp.einsum('qk,qd->kd', grad_scores, query, preferred_element_type=jnp.fl...]
    all_to_all x2 -> x0, starting transfers between devices: 7.74 us -> none  [the longest x1 4.18 us: body(): lax.all_to_all(fanned, ('section', 'doc'), split_axis=0, concat_axis=0, t...]
    unnamed x4 -> x15, local copies, waits for them, and re-layouts: 0.01 us -> 7.03 us
    all_gather x1 -> x0, blocking collectives: 5.44 us -> none  [body(): lax.all_gather(doc_lists, 'doc', axis=0, tiled=True)]
    dynamic_slice x8 -> x0, local copies, waits for them, and re-layouts: 3.91 us -> none  [body(): lax.map(row_attention, (queries, cotangent, memory))]
  transfers between devices with their start and end apart: 2 -> 0, of which waited for: 2 -> 0; matrix products, arithmetic and copies ran while one was open for 0% -> 0% of each run, Pallas kernels for 0% -> 0%
where the time goes in v1:
time: 54.3 us; the launch traced here: 54 us
  Pallas kernels  46.3 us (85%)
  local copies, waits for them, and re-layouts  7.03 us (13%)
  between operations  0.66 us (1%)
    pallas_call x1, Pallas kernels, body(): pl.pallas_call(functools.partial(kernel, cfg), out_shape=(jax.ShapeDtypeS...  46.3 us
    unnamed x15, local copies, waits for them, and re-layouts  7.03 us

profile of v1, /device:TPU:0, one launch (start us, length us, event | category | flops | bytes accessed | tf_op | source)
XLA Modules:
  0.0 54.0 jit_solution(15468055889031715673)
XLA Ops:
  0.6 0.0 copy-start.4
  0.6 0.0 copy-start.5
  0.7 0.7 %copy-done.4 = s32[2,8]{1,0:T(2,128)S(1)} copy-done((s32[2,8]{1,0:T(2,128)S(1)}, s32[2,8]{1,0:T(2,128)}, u32[]{:S(2)}) %copy-start.4) | copy-done | bytes 88
  1.3 0.0 copy-done.5
  1.3 0.0 copy-start
  1.3 1.0 %copy-done = bf16[2,512,2,1,128]{4,2,3,1,0:T(2,128)(2,1)S(1)} copy-done((bf16[2,512,2,1,128]{4,2,3,1,0:T(2,128)(2,1)S(1)}, bf16[2,512,2,1,128]{4,2,3,1,0:T(2,128)(2,1)}, u32[]{:S(2)}) %copy-start) | copy-done | bytes 524312
  2.4 0.0 copy-start.1
  2.4 1.0 %copy-done.1 = bf16[2,512,2,1,128]{4,2,3,1,0:T(2,128)(2,1)S(1)} copy-done((bf16[2,512,2,1,128]{4,2,3,1,0:T(2,128)(2,1)S(1)}, bf16[2,512,2,1,128]{4,2,3,1,0:T(2,128)(2,1)}, u32[]{:S(2)}) %copy-start.1) | copy-done | bytes 524312
  3.4 0.0 copy-start.2
  3.4 1.0 %copy-done.2 = f32[16,32,1,2,128]{4,3,2,1,0:T(2,128)S(1)} copy-done((f32[16,32,1,2,128]{4,3,2,1,0:T(2,128)S(1)}, f32[16,32,1,2,128]{4,3,2,1,0:T(2,128)}, u32[]{:S(2)}) %copy-start.2) | copy-done | bytes 524312
  4.4 0.0 copy-start.3
  4.4 0.9 %copy-done.3 = bf16[16,32,1,2,128]{4,3,2,1,0:T(2,128)(2,1)S(1)} copy-done((bf16[16,32,1,2,128]{4,3,2,1,0:T(2,128)(2,1)S(1)}, bf16[16,32,1,2,128]{4,3,2,1,0:T(2,128)(2,1)}, u32[]{:S(2)}) %copy-start.3) | copy-done | bytes 262168
  5.4 46.3 %shard_map.85 = (bf16[2,1024,128]{2,1,0:T(8,128)(2,1)S(1)}, bf16[1024,128]{1,0:T(8,128)(2,1)S(1)}, f32[1024,128]{1,0:T(8,128)S(1)}) custom-call(s32[2,8]{1,0:T(2,128)S(1)} %copy-done.4, s32[32]{0:T(128)S(1)} %copy-done.5, bf16[2,1024,128]{2,1,0:T(8,128)(2,1)S(1)} %bitcast.16, bf16[2,1024,128]{2,1,0:T(8,128)(2,1)S(1)} %bitcast.17, ...), custom_call_target="tpu_custom_call" | custom-call | flops 2684354560 | bytes 4194304 | tf_op jit(solution)/shard_map/pallas_call | solution.py:321
  51.7 0.8 %copy.15 = bf16[2,512,2,1,128]{4,2,3,1,0:T(2,128)(2,1)} copy(bf16[2,512,2,1,128]{4,2,3,1,0:T(2,128)(2,1)S(1)} %bitcast.14) | data formatting | bytes 1048576
  52.5 0.7 %copy.16 = bf16[16,32,1,2,128]{4,3,2,1,0:T(2,128)(2,1)} copy(bf16[16,32,1,2,128]{4,3,2,1,0:T(2,128)(2,1)S(1)} %bitcast.15) | data formatting | bytes 524288
  53.2 0.8 %copy.17 = f32[16,32,1,2,128]{4,3,2,1,0:T(2,128)} copy(f32[16,32,1,2,128]{4,3,2,1,0:T(2,128)S(1)} %bitcast.13) | data formatting | bytes 1048576
Async XLA Ops:
  0.6 0.7 %copy-start.4 = (s32[2,8]{1,0:T(2,128)S(1)}, s32[2,8]{1,0:T(2,128)}, u32[]{:S(2)}) copy-start(s32[2,8]{1,0:T(2,128)} %lists_ref.1) | copy-start | bytes 196
  0.6 0.7 %copy-start.5 = (s32[32]{0:T(128)S(1)}, s32[32]{0:T(128)}, u32[]{:S(2)}) copy-start(s32[32]{0:T(128)} %place_ref.1) | copy-start | bytes 388
  1.3 1.0 %copy-start = (bf16[2,512,2,1,128]{4,2,3,1,0:T(2,128)(2,1)S(1)}, bf16[2,512,2,1,128]{4,2,3,1,0:T(2,128)(2,1)}, u32[]{:S(2)}) copy-start(bf16[2,512,2,1,128]{4,2,3,1,0:T(2,128)(2,1)} %param.6) | copy-start | bytes 1572868
  2.4 1.0 %copy-start.1 = (bf16[2,512,2,1,128]{4,2,3,1,0:T(2,128)(2,1)S(1)}, bf16[2,512,2,1,128]{4,2,3,1,0:T(2,128)(2,1)}, u32[]{:S(2)}) copy-start(bf16[2,512,2,1,128]{4,2,3,1,0:T(2,128)(2,1)} %param.7) | copy-start | bytes 1572868
  3.4 1.0 %copy-start.2 = (f32[16,32,1,2,128]{4,3,2,1,0:T(2,128)S(1)}, f32[16,32,1,2,128]{4,3,2,1,0:T(2,128)}, u32[]{:S(2)}) copy-start(f32[16,32,1,2,128]{4,3,2,1,0:T(2,128)} %param.9) | copy-start | bytes 1572868
  4.4 0.9 %copy-start.3 = (bf16[16,32,1,2,128]{4,3,2,1,0:T(2,128)(2,1)S(1)}, bf16[16,32,1,2,128]{4,3,2,1,0:T(2,128)(2,1)}, u32[]{:S(2)}) copy-start(bf16[16,32,1,2,128]{4,3,2,1,0:T(2,128)(2,1)} %param.8) | copy-start | bytes 786436

commit v2 on v1

v2 whole, which is shorter than its diff:
```python
import functools
import math

import jax
import jax.numpy as jnp
from jax import lax
from jax.experimental import pallas as pl
from jax.experimental.pallas import tpu as pltpu
from jax.sharding import PartitionSpec as P

momentum_decay = 0.9
step_rate = 0.3
clip_level = 0.5
MESH = pl.DeviceIdType.MESH


def nt(a, b):
    return lax.dot_general(a, b, (((1,), (1,)), ((), ())), preferred_element_type=jnp.float32)


def mm(a, b):
    return jnp.dot(a, b, preferred_element_type=jnp.float32)


def kernel(
    cfg,
    lists_ref, place_ref, q_hbm, t_hbm, cache_hbm, mom_hbm,
    att_hbm, newc_ref, newm_ref,
    allpos, tab, target, inverse,
    q_ref, t_ref, att_ref, cache_ref, mom_ref,
    posvm, wide, kvc, arr_k, arr_v, outbuf, keys, vals, valt, wts, dkv,
    keep, snd, rcv_k, rcv_v, parcel, ret, parts,
    in_sem, out_sem, pos_send, pos_recv, loc_sem, dir_send, arr_recv, fwd_send,
    sib_send, sib_recv, ret_send, ret_recv, n_send, n_recv,
):
    sections, owners, mps, cap, doc_dev, len_part, rows, list_len, clip_limit, score_scale = cfg
    arr, rcv = (arr_k, arr_v), (rcv_k, rcv_v)
    low = 2 if sections % 2 == 0 else 1
    high = sections // low
    requests = rows * list_len
    head = q_ref.shape[-1]
    sec = lax.axis_index("section")
    doc = lax.axis_index("doc")
    mp = lax.axis_index("mp")
    hi = sec // low
    lo = sec % low
    everyone = sections * owners * mps
    me = (sec * owners + doc) * mps + mp

    def rot(base, step, size):
        return lax.rem(base + step, size)

    def device(n):
        return {"section": n // (owners * mps), "doc": (n // mps) % owners, "mp": n % mps}

    peers = [(a, b) for a in range(high) for b in range(owners) if (a, b) != (0, 0)]
    loads = [
        pltpu.make_async_copy(src, dst, in_sem.at[n])
        for n, (src, dst) in enumerate(
            ((cache_hbm, cache_ref), (q_hbm, q_ref), (t_hbm, t_ref), (mom_hbm, mom_ref))
        )
    ]
    leaves = [
        pltpu.make_async_copy(att_ref.at[row], att_hbm.at[row], out_sem.at[row]) for row in range(rows)
    ]
    loads[0].start()
    barrier = pltpu.get_barrier_semaphore()

    def greet(n, carry):
        pl.semaphore_signal(barrier, inc=1, device_id=device(rot(me, n, everyone)), device_id_type=MESH)
        return carry

    lax.fori_loop(1, everyone, greet, 0)
    for load in loads[1:]:
        load.start()

    def to(s, d):
        return {"section": s, "doc": d, "mp": mp}

    def remote(src, dst, ssem, rsem, dev):
        return pltpu.make_async_remote_copy(
            src_ref=src, dst_ref=dst, send_sem=ssem, recv_sem=rsem, device_id=dev,
            device_id_type=MESH,
        )

    lane = lax.broadcasted_iota(jnp.int32, (8, 128), 1)
    vec = jnp.zeros((8, 128), jnp.int32)
    places = []
    for r in range(requests):
        where = place_ref[lists_ref[r // list_len, r % list_len]]
        places.append(where)
        vec = jnp.where(lane == r, where, vec)
    posvm[doc] = vec

    def slots(get, d):
        found = [jnp.int32(-1)] * cap
        seen = jnp.int32(0)
        for r in range(requests):
            where = get(r)
            mine = (where // doc_dev) == doc
            local = where % doc_dev
            for c in range(min(cap, r + 1)):
                found[c] = jnp.where(mine & (seen == c), local, found[c])
            seen = seen + mine.astype(jnp.int32)
        for c in range(cap):
            tab[d * cap + c] = found[c]
        return found

    found = slots(lambda r: places[r], doc)

    loads[0].wait()
    count = doc_dev * len_part
    wide[0 : 2 * count, :] = cache_ref[...].astype(jnp.float32)
    for kv in range(2):
        kvc[kv] = wide[pl.ds(kv, count, stride=2), :].astype(jnp.bfloat16).reshape(doc_dev, len_part, head)
    for kv in range(2):
        for c in range(cap):
            arr[kv][sec, doc * cap + c] = kvc[kv, jnp.maximum(found[c], 0)]

    pl.semaphore_wait(barrier, everyone - 1)

    sends = []

    def send(src, dst, ssem, rsem, dev):
        cp = remote(src, dst, ssem, rsem, dev)
        cp.start()
        sends.append(cp)

    for b in range(1, owners):
        send(posvm.at[doc], posvm.at[doc], pos_send.at[b], pos_recv.at[doc], to(sec, rot(doc, b, owners)))

    sib = hi * low + rot(lo, 1, low)

    def block(kv, s, d):
        return arr[kv].at[s, pl.ds(d * cap, cap)]

    def forward(kv, h, d):
        if low == 1:
            return
        s = h * low + lo
        send(block(kv, s, d), block(kv, s, d), fwd_send.at[kv, h, d], arr_recv.at[kv, s, d], to(sib, doc))

    def arrive(kv, s, d):
        remote(block(kv, s, d), block(kv, s, d), dir_send.at[kv, 0, 0], arr_recv.at[kv, s, d], to(s, d)).wait_recv()

    for kv in range(2):
        for a in range(1, high):
            h = rot(hi, a, high)
            send(block(kv, sec, doc), block(kv, sec, doc), dir_send.at[kv, a, 0], arr_recv.at[kv, sec, doc], to(h * low + lo, doc))
    for kv in range(2):
        forward(kv, hi, doc)

    for b in range(1, owners):
        d = rot(doc, b, owners)
        remote(posvm.at[d], posvm.at[d], pos_send.at[b], pos_recv.at[d], to(sec, d)).wait_recv()
        local = pltpu.make_async_copy(posvm.at[d], allpos.at[d], loc_sem)
        local.start()
        local.wait()
        found = slots(lambda r: allpos[d, 0, r], d)
        for kv in range(2):
            for c in range(cap):
                outbuf[kv, b, c] = kvc[kv, jnp.maximum(found[c], 0)]
            for a in range(high):
                h = rot(hi, a, high)
                send(outbuf.at[kv, b], block(kv, sec, doc), dir_send.at[kv, a, b], arr_recv.at[kv, sec, doc], to(h * low + lo, d))

    targets = []
    for r in range(requests):
        rank = jnp.int32(0)
        for e in range(r):
            rank = rank + ((places[e] // doc_dev) == (places[r] // doc_dev)).astype(jnp.int32)
        targets.append((places[r] // doc_dev) * cap + rank)
        target[r] = targets[r]
    for i in range(owners * cap):
        who = jnp.int32(0)
        for r in range(requests):
            who = jnp.where(targets[r] == i, r, who)
        inverse[i] = who

    def relay(kv):
        for a, b in peers:
            h, d = rot(hi, a, high), rot(doc, b, owners)
            arrive(kv, h * low + lo, d)
            forward(kv, h, d)

    def relayed(kv):
        if low > 1:
            for a in range(high):
                for b in range(owners):
                    arrive(kv, rot(hi, a, high) * low + rot(lo, 1, low), rot(doc, b, owners))

    def assemble(kv, row, dst):
        for i in range(list_len):
            slot = target[row * list_len + i]
            for s in range(sections):
                at = (i * sections + s) * len_part
                dst[at : at + len_part, :] = arr[kv][s, slot]

    exp_scale = score_scale * math.log2(math.e)
    shape5 = (list_len, high, low, len_part, head)

    def share(kv, row, value):
        dkv[kv] = value.reshape(shape5)
        span = pl.ds(row * list_len, list_len)
        for h in range(high):
            keep[kv, span, h] = dkv[kv, :, h, lo]
            if low > 1:
                snd[kv, span, h] = dkv[kv, :, h, rot(lo, 1, low)].astype(jnp.bfloat16)
        if low > 1:
            send(snd.at[kv, span], rcv[kv].at[span], sib_send.at[kv, row], sib_recv.at[kv, row], to(sib, doc))

    def slot_block(kv, h, d):
        return ret.at[kv, h, pl.ds(d * cap, cap)]

    def give_back(kv):
        if low > 1:
            for row in range(rows):
                span = pl.ds(row * list_len, list_len)
                remote(snd.at[kv, span], rcv[kv].at[span], sib_send.at[kv, row], sib_recv.at[kv, row], to(sib, doc)).wait_recv()

        def total(request, h):
            value = keep[kv, request, h]
            if low > 1:
                value = value + rcv[kv][request, h].astype(jnp.float32)
            return value.astype(jnp.bfloat16)

        for a, b in peers[::-1]:
            h, d = rot(hi, a, high), rot(doc, b, owners)
            for c in range(cap):
                parcel[kv, a, b, c] = total(inverse[d * cap + c], h)
            send(parcel.at[kv, a, b], slot_block(kv, hi, doc), ret_send.at[kv, a, b], ret_recv.at[kv, hi, doc], to(h * low + lo, d))
        for c in range(cap):
            ret[kv, hi, doc * cap + c] = total(inverse[doc * cap + c], hi)

    def first_half(row):
        assemble(0, row, keys.at[row])
        scores = nt(keys[row], q_ref[row])
        top = jnp.max(scores, axis=0, keepdims=True)
        power = jnp.exp2((scores - top) * exp_scale)
        weights = power * (1.0 / jnp.sum(power, axis=0, keepdims=True))
        wts[row] = weights.astype(jnp.bfloat16)
        share(1, row, mm(wts[row], t_ref[row]))

    def second_half(row):
        assemble(1, row, vals)
        valt[...] = vals[...].T
        t = t_ref[row]
        attended = mm(valt[...], wts[row]).astype(jnp.bfloat16).astype(jnp.float32)
        att_ref[row] = attended.T.astype(jnp.bfloat16)
        leaves[row].start()
        delta = jnp.sum(attended * t.astype(jnp.float32).T, axis=0, keepdims=True)
        grad = (wts[row].astype(jnp.float32) * (nt(vals[...], t) - delta)).astype(jnp.bfloat16)
        share(0, row, mm(grad, q_ref[row]) * score_scale)

    relay(0)
    for load in loads[1:]:
        load.wait()
    relayed(0)
    for row in range(rows):
        first_half(row)
        if row == 0:
            relay(1)
    relayed(1)
    for row in range(rows):
        second_half(row)
        if row == 0:
            give_back(1)
    give_back(0)
    for kv in (1, 0):
        for a, b in peers:
            h, d = rot(hi, a, high), rot(doc, b, owners)
            remote(parcel.at[kv, a, b], slot_block(kv, h, d), ret_send.at[kv, a, b], ret_recv.at[kv, h, d], to(h * low + lo, d)).wait_recv()

    def gather(p, square):
        base = p * 2 * len_part
        value = [jnp.zeros((len_part, head), jnp.float32)] * 2
        for d in range(owners):
            pick = jnp.int32(0)
            named = jnp.float32(0.0)
            for c in range(cap):
                same = tab[d * cap + c] == p
                pick = jnp.where(same, c, pick)
                named = jnp.where(same, jnp.float32(1.0), named)
            for kv in range(2):
                both = ret[kv, 0, d * cap + pick].astype(jnp.float32)
                for h in range(1, high):
                    both = both + ret[kv, h, d * cap + pick].astype(jnp.float32)
                value[kv] = value[kv] + jnp.where(named > 0.5, both, 0.0)
        for kv in range(2):
            wide[pl.ds(base + kv, len_part, stride=2), :] = value[kv]
            square = square + jnp.sum((value[kv] * value[kv]).reshape(-1, 8, head), axis=0)
        return square

    square = lax.fori_loop(0, doc_dev, gather, jnp.zeros((8, head), jnp.float32))

    parts[me] = square

    def tell(n, carry):
        remote(parts.at[me], parts.at[me], n_send.at[n], n_recv.at[me], device(rot(me, n, everyone))).start()
        return carry

    def hear(n, carry):
        other = rot(me, n, everyone)
        remote(parts.at[other], parts.at[other], n_send.at[n], n_recv.at[other], device(other)).wait_recv()
        return carry

    def told(n, carry):
        remote(parts.at[me], parts.at[me], n_send.at[n], n_recv.at[me], device(rot(me, n, everyone))).wait_send()
        return carry

    lax.fori_loop(1, everyone, tell, 0)
    newm_ref[...] = momentum_decay * mom_ref[...]
    for cp in sends:
        cp.wait_send()
    for leave in leaves:
        leave.wait()
    lax.fori_loop(1, everyone, hear, 0)
    whole = jnp.sum(parts[...], axis=0)
    whole = jnp.sum(jnp.sum(whole, axis=0, keepdims=True), axis=1, keepdims=True)
    factor = clip_limit / jnp.maximum(jnp.sqrt(whole), clip_limit)
    fresh = newm_ref[...] + factor * wide[0 : 2 * count, :]
    newm_ref[...] = fresh
    newc_ref[...] = (cache_ref[...].astype(jnp.float32) - step_rate * fresh).astype(jnp.bfloat16)
    lax.fori_loop(1, everyone, told, 0)


def body(queries, cotangent, cache, momentum, doc_lists, place):
    rows, seq_len, heads, kv_count, head = queries.shape
    doc_dev, len_part = cache.shape[:2]
    doc_total = place.shape[0]
    owners = doc_total // doc_dev
    sections = lax.axis_size("section")
    mps = lax.axis_size("mp")
    list_len = doc_lists.shape[1]
    requests = rows * list_len
    used = min(owners, requests)
    cap = (requests + used - 1) // used
    low = 2 if sections % 2 == 0 else 1
    high = sections // low
    entry_count = doc_total * len_part * sections * kv_count * mps * 2 * head
    clip_limit = clip_level * math.sqrt(entry_count)
    cfg = (sections, owners, mps, cap, doc_dev, len_part, rows, list_len, clip_limit, 1.0 / math.sqrt(head))
    f32, bf16, i32 = jnp.float32, jnp.bfloat16, jnp.int32
    key_count = list_len * sections * len_part
    flat = 2 * doc_dev * len_part
    vm, dma = pltpu.VMEM, pltpu.SemaphoreType.DMA
    shape5 = (list_len, high, low, len_part, head)
    piece = (len_part, head)
    everyone = sections * owners * mps
    hbm = pl.BlockSpec(memory_space=pltpu.HBM)
    vmem = pl.BlockSpec(memory_space=pltpu.VMEM)
    smem = pl.BlockSpec(memory_space=pltpu.SMEM)
    queries_flat = queries.reshape(rows, seq_len * heads, head)
    att, newc, newm = pl.pallas_call(
        functools.partial(kernel, cfg),
        out_shape=(
            jax.ShapeDtypeStruct(queries_flat.shape, bf16),
            jax.ShapeDtypeStruct((flat, head), bf16),
            jax.ShapeDtypeStruct((flat, head), f32),
        ),
        in_specs=[smem, smem, hbm, hbm, hbm, hbm],
        out_specs=(hbm, vmem, vmem),
        scratch_shapes=[
            pltpu.SMEM((owners, 8, 128), i32),
            pltpu.SMEM((owners * cap,), i32),
            pltpu.SMEM((requests,), i32),
            pltpu.SMEM((owners * cap,), i32),
            vm(queries_flat.shape, bf16),
            vm(queries_flat.shape, bf16),
            vm(queries_flat.shape, bf16),
            vm((flat, head), bf16),
            vm((flat, head), f32),
            vm((owners, 8, 128), i32),
            vm((flat + 8, head), f32),
            vm((2, doc_dev) + piece, bf16),
            vm((sections, owners * cap) + piece, bf16),
            vm((sections, owners * cap) + piece, bf16),
            vm((2, owners, cap) + piece, bf16),
            vm((rows, key_count, head), bf16),
            vm((key_count, head), bf16),
            vm((head, key_count), bf16),
            vm((rows, key_count, seq_len * heads), bf16),
            vm((2,) + shape5, f32),
            vm((2, requests, high) + piece, f32),
            vm((2, requests, high) + piece, bf16),
            vm((requests, high) + piece, bf16),
            vm((requests, high) + piece, bf16),
            vm((2, high, owners, cap) + piece, bf16),
            vm((2, high, owners * cap) + piece, bf16),
            vm((everyone, 8, head), f32),
            dma((4,)),
            dma((rows,)),
            dma((owners,)),
            dma((owners,)),
            dma,
            dma((2, high, owners)),
            dma((2, sections, owners)),
            dma((2, high, owners)),
            dma((2, rows)),
            dma((2, rows)),
            dma((2, high, owners)),
            dma((2, high, owners)),
            dma((everyone,)),
            dma((everyone,)),
        ],
        compiler_params=pltpu.CompilerParams(
            collective_id=0, has_side_effects=True, vmem_limit_bytes=56 * 1024 * 1024
        ),
        cost_estimate=pl.CostEstimate(
            flops=10 * rows * seq_len * heads * key_count * head,
            bytes_accessed=4 * 1024 * 1024,
            transcendentals=rows * seq_len * heads * key_count,
        ),
    )(
        doc_lists,
        place,
        queries_flat,
        cotangent.reshape(queries_flat.shape),
        cache.reshape(flat, head),
        momentum.reshape(flat, head),
    )
    return att.reshape(queries.shape), newc.reshape(cache.shape), newm.reshape(momentum.shape)


def solution(mesh):
    in_specs = (
        P("doc", None, "section", "mp", None),
        P("doc", None, "section", "mp", None),
        P("doc", "section", "mp", None, None),
        P("doc", "section", "mp", None, None),
        P("doc", None),
        P(),
    )
    out_specs = (
        P("doc", None, "section", "mp", None),
        P("doc", "section", "mp", None, None),
        P("doc", "section", "mp", None, None),
    )
    return jax.shard_map(body, mesh=mesh, in_specs=in_specs, out_specs=out_specs, check_vma=False)
```

time: 54.3 us -> 45.4 us (0.84)
  Pallas kernels: 46.3 us -> 40.4 us
  local copies, waits for them, and re-layouts: 7.03 us -> 4.17 us
    pallas_call x1, Pallas kernels: 46.3 us -> 40.4 us  [body(): pl.pallas_call(functools.partial(kernel, cfg), out_shape=(jax.ShapeDtypeS...]
    unnamed x15 -> x7, local copies, waits for them, and re-layouts: 7.03 us -> 4.17 us
where the time goes in v2:
time: 45.4 us; the launch traced here: 45.2 us
  Pallas kernels  40.4 us (89%)
  local copies, waits for them, and re-layouts  4.17 us (9%)
  between operations  0.65 us (1%)
    pallas_call x1, Pallas kernels, body(): pl.pallas_call(functools.partial(kernel, cfg), out_shape=(jax.ShapeDtypeS...  40.4 us
    unnamed x7, local copies, waits for them, and re-layouts  4.17 us

profile of v2, /device:TPU:0, one launch (start us, length us, event | category | flops | bytes accessed | tf_op | source)
XLA Modules:
  0.0 45.2 jit_solution(6942865648063977524)
XLA Ops:
  0.6 40.4 %shard_map.85 = (bf16[2,1024,128]{2,1,0:T(8,128)(2,1)}, bf16[1024,128]{1,0:T(8,128)(2,1)}, f32[1024,128]{1,0:T(8,128)}) custom-call(s32[2,8]{1,0:T(2,128)} %lists_ref.1, s32[32]{0:T(128)} %place_ref.1, bf16[2,1024,128]{2,1,0:T(8,128)(2,1)} %bitcast.16, bf16[2,1024,128]{2,1,0:T(8,128)(2,1)} %bitcast.17, bf16[1024,128]{1,0:T(8,128)(2,1)} %bitcast.19, ...), custom_call_target="tpu_custom_call" | custom-call | flops 2684354560 | bytes 4194304 | tf_op jit(solution)/shard_map/pallas_call | solution.py:354
  41.0 0.0 copy-start.1
  41.0 2.2 %copy.15 = bf16[2,512,2,1,128]{4,2,3,1,0:T(2,128)(2,1)} copy(bf16[2,512,2,1,128]{4,2,3,1,0:T(2,128)(2,1)} %bitcast.14) | data formatting | bytes 1048576
  43.3 0.0 copy-done.1
  43.3 0.0 copy-start
  43.3 0.7 %copy.16 = bf16[16,32,1,2,128]{4,3,2,1,0:T(2,128)(2,1)} copy(bf16[16,32,1,2,128]{4,3,2,1,0:T(2,128)(2,1)S(1)} %bitcast.15) | data formatting | bytes 524288
  44.0 0.4 copy-done
  44.4 0.8 %copy.17 = f32[16,32,1,2,128]{4,3,2,1,0:T(2,128)} copy(f32[16,32,1,2,128]{4,3,2,1,0:T(2,128)S(1)} %bitcast.13) | data formatting | bytes 1048576
Async XLA Ops:
  41.0 2.2 %copy-start.1 = (bf16[1024,128]{1,0:T(8,128)(2,1)S(1)}, bf16[1024,128]{1,0:T(8,128)(2,1)}, u32[]{:S(2)}) copy-start(bf16[1024,128]{1,0:T(8,128)(2,1)} %get-tuple-element.7) | copy-start | bytes 786436
  43.3 1.1 %copy-start = (f32[1024,128]{1,0:T(8,128)S(1)}, f32[1024,128]{1,0:T(8,128)}, u32[]{:S(2)}) copy-start(f32[1024,128]{1,0:T(8,128)} %get-tuple-element.8) | copy-start | bytes 1572868
